TPU v7x, 32 devices: a whole 2x2x4 slice. The times are simulated.
32 devices in a mesh: ctx: 8 (over y, x, core), tp: 4 (over z).
Axes of the slice: x: 2, y: 2, z: 4, core: 2. Of those that a mesh axis runs over, the one named last changes fastest.
Arguments:
- queries: bfloat16 [8192, 8192], P(('ctx', 'tp')), may hold values from -36 to 36
- key_rows: bfloat16 [8192, 1024], P(('ctx', 'tp')), may hold values from -6 to 6
- value_rows: bfloat16 [8192, 1024], P(('ctx', 'tp')), may hold values from -6 to 6
- vertical_keys: int32 [8, 1024], P('tp'), may hold values from 0 to 8191, as said below
- slash_offsets: int32 [8, 3], P('tp'), may hold values from 0 to 8128, as said below
Outputs:
- attended: bfloat16 [8192, 8192], P('ctx', 'tp')
Inputs may be any that keep to these rules, and one draw needn't show every extreme that they name: `vertical_keys`: each row holds 1024 distinct positions in ascending order; no more than 384 of a row lie in one aligned range of 1024 positions, and in every row some such range holds exactly 384. `slash_offsets`: each row holds 3 distinct multiples of 64, the first of them 0.
All inputs are finite; a program needn't handle non-finite values.
Results may differ from a plain program's by a relative error of at most 0.0035.
Values may be sent and summed in bfloat16 or wider, within the bound.
A program may use at most 320 MiB of HBM per device.

v0:
```python
import functools
import math

import jax
import jax.numpy as jnp
from jax import lax
from jax.experimental import pallas as pl
from jax.experimental.pallas import tpu as pltpu
from jax.sharding import PartitionSpec as P

HQ = 64
KVH = 8
DH = 128
SUB = 64
CHUNKS = 4
VT = 128
PB = 512
EXP2_SCALE = DH**-0.5 * math.log2(math.e)
MASKED = -1e30
VMEM_BYTES = 56 * 1024 * 1024


def gather_body(tok, me_ref, keys_ref, column_ref, kv_ref, vk_ref, vv_ref, marks_ref):
    me = me_ref[0]
    marks_ref[...] = jnp.zeros_like(marks_ref)
    lanes = lax.broadcasted_iota(jnp.int32, (VT, PB), 1)
    for tile in range(keys_ref.shape[0] // VT):
        first = keys_ref[tile * VT] // PB
        last = keys_ref[tile * VT + VT - 1] // PB
        column = column_ref[tile * VT : (tile + 1) * VT, :]

        def add_block(block, total):
            base = block * PB
            place = (lax.bitwise_xor(base // tok, me)) * tok + base % tok
            rows = kv_ref[pl.ds(pl.multiple_of(place, PB), PB), :]
            hit = jnp.where(column - base == lanes, 1.0, 0.0)
            marks_ref[pl.ds(block, 1), :] += jnp.sum(hit, axis=0, keepdims=True)
            return total + jnp.dot(
                hit.astype(jnp.bfloat16), rows, preferred_element_type=jnp.float32
            )

        total = lax.fori_loop(first, last + 1, add_block, jnp.zeros((VT, 2 * DH), jnp.float32))
        total = total.astype(jnp.bfloat16)
        vk_ref[tile * VT : (tile + 1) * VT, :] = total[:, :DH]
        vv_ref[tile * VT : (tile + 1) * VT, :DH] = total[:, DH:]
        vv_ref[tile * VT : (tile + 1) * VT, DH:] = jnp.ones((VT, DH), jnp.bfloat16)


def gather_vertical(me, keys, kv, tok):
    vert = keys.shape[0]
    total = kv.shape[0]
    return pl.pallas_call(
        functools.partial(gather_body, tok),
        out_shape=(
            jax.ShapeDtypeStruct((vert, DH), jnp.bfloat16),
            jax.ShapeDtypeStruct((vert, 2 * DH), jnp.bfloat16),
            jax.ShapeDtypeStruct((total // PB, PB), jnp.float32),
        ),
        in_specs=[
            pl.BlockSpec(memory_space=pltpu.SMEM),
            pl.BlockSpec(memory_space=pltpu.SMEM),
            pl.BlockSpec(memory_space=pltpu.VMEM),
            pl.BlockSpec(memory_space=pltpu.VMEM),
        ],
        out_specs=[pl.BlockSpec(memory_space=pltpu.VMEM)] * 3,
        compiler_params=pltpu.CompilerParams(vmem_limit_bytes=VMEM_BYTES),
        cost_estimate=pl.CostEstimate(flops=8 << 30, bytes_accessed=8 << 20, transcendentals=0),
        name="gather_vertical",
    )(me, keys, keys[:, None], kv)


def attend_body(tok, bands, group, meta_ref, q_ref, row_ref, vk_ref, vv_ref, kv_ref, marks_ref, *rest):
    o_ref = rest[-1]
    me = meta_ref[0]
    per_dev = tok // SUB
    rows = group * SUB
    slots = 4 * SUB
    row_in = lax.broadcasted_iota(jnp.int32, (rows, slots), 0) % SUB
    lane_in = lax.broadcasted_iota(jnp.int32, (rows, slots), 1) % SUB
    upper = lane_in > row_in
    ones = jnp.ones((slots, DH), jnp.bfloat16)
    nt = (((1,), (1,)), ((), ()))
    subs = q_ref.shape[0] // SUB
    for sub in range(subs):
        own = me * per_dev + pl.program_id(0) * subs + sub
        sides = []
        for back in (1, 0):
            blocks, biases = [], []
            for band in range(bands):
                block = own - meta_ref[1 + band] - back
                there = jnp.maximum(block, 0)
                place = lax.bitwise_xor(there // per_dev, me) * per_dev + there % per_dev
                blocks.append(kv_ref[pl.ds(pl.multiple_of(place * SUB, SUB), SUB), :])
                if band == 0 and back == 0:
                    biases.append(jnp.zeros((1, SUB), jnp.float32))
                else:
                    gone = (marks_ref[pl.ds(there, 1), :] > 0.5) | (block < 0)
                    biases.append(jnp.where(gone, MASKED, 0.0))
            for _ in range(4 - bands):
                blocks.append(jnp.zeros((SUB, 2 * DH), jnp.bfloat16))
                biases.append(jnp.full((1, SUB), MASKED, jnp.float32))
            sides.append((jnp.concatenate(blocks, axis=0), jnp.concatenate(biases, axis=1)))
        (near, near_bias), (own_side, own_bias) = sides
        q = jnp.concatenate(
            [q_ref[sub * SUB : (sub + 1) * SUB, g * DH : (g + 1) * DH] for g in range(group)], axis=0
        )
        vert_bias = jnp.where(row_ref[...] < own * SUB, 0.0, MASKED)
        vert = (
            lax.dot_general(q, vk_ref[...], nt, preferred_element_type=jnp.float32) + vert_bias
        )
        s_near = lax.dot_general(q, near[:, :DH], nt, preferred_element_type=jnp.float32)
        s_own = lax.dot_general(q, own_side[:, :DH], nt, preferred_element_type=jnp.float32)
        band = jnp.where(upper, s_near + near_bias, s_own + own_bias)
        top = jnp.maximum(
            jnp.max(vert, axis=1, keepdims=True), jnp.max(band, axis=1, keepdims=True)
        )
        p_vert = jnp.exp2((vert - top) * EXP2_SCALE).astype(jnp.bfloat16)
        p_band = jnp.exp2((band - top) * EXP2_SCALE)
        p_near = jnp.where(upper, p_band, 0.0).astype(jnp.bfloat16)
        p_own = jnp.where(upper, 0.0, p_band).astype(jnp.bfloat16)
        acc = jnp.dot(p_vert, vv_ref[...], preferred_element_type=jnp.float32)
        acc += jnp.dot(
            p_near,
            jnp.concatenate((near[:, DH:], ones), axis=1),
            preferred_element_type=jnp.float32,
        )
        acc += jnp.dot(
            p_own,
            jnp.concatenate((own_side[:, DH:], ones), axis=1),
            preferred_element_type=jnp.float32,
        )
        out = (acc[:, :DH] / acc[:, DH:]).astype(o_ref.dtype)
        for g in range(group):
            o_ref[sub * SUB : (sub + 1) * SUB, g * DH : (g + 1) * DH] = out[
                g * SUB : (g + 1) * SUB
            ]


def attend(meta, q, row, vk, vv, kv, marks, previous, chunk, bands, width):
    tok, columns = q.shape
    group = columns // DH
    block = 128

    def whole(x):
        return pl.BlockSpec(x.shape, lambda i, meta_ref: (0, 0))

    operands = [meta, q, row, vk, vv, kv, marks]
    in_specs = [pl.BlockSpec((block, columns), lambda i, meta_ref: (i, 0))]
    in_specs += [whole(x) for x in operands[2:]]
    aliases = {}
    if previous is not None:
        aliases = {len(operands): 0}
        operands.append(previous)
        in_specs.append(pl.BlockSpec(memory_space=pl.ANY))
    scores = tok * group * 1536
    return pl.pallas_call(
        functools.partial(attend_body, tok, bands, group),
        out_shape=jax.ShapeDtypeStruct((tok, width), jnp.bfloat16),
        grid_spec=pltpu.PrefetchScalarGridSpec(
            num_scalar_prefetch=1,
            grid=(tok // block,),
            in_specs=in_specs,
            out_specs=pl.BlockSpec((block, columns), lambda i, meta_ref: (i, chunk)),
        ),
        input_output_aliases=aliases,
        compiler_params=pltpu.CompilerParams(vmem_limit_bytes=VMEM_BYTES),
        cost_estimate=pl.CostEstimate(
            flops=scores * 1536, bytes_accessed=8 << 20, transcendentals=scores
        ),
        name=f"attend_{chunk}",
    )(*operands)


def gather_ctx(block, order):
    count = lax.axis_size("ctx")
    held = block[None]
    for bit in order:
        route = [(i, i ^ (1 << bit)) for i in range(count)]
        held = jnp.concatenate((held, lax.ppermute(held, "ctx", route)), axis=0)
    bits = len(order)
    held = held.reshape((2,) * bits + block.shape)
    steps = list(reversed(order))
    axes = [steps.index(bit) for bit in reversed(range(bits))]
    held = held.transpose(axes + [bits, bits + 1])
    return held.reshape(count * block.shape[0], block.shape[1])


def shards(queries, key_rows, value_rows, vertical_keys, slash_offsets):
    heads, vert_count = vertical_keys.shape
    bands = slash_offsets.shape[1]
    part = queries.shape[0]
    tp = lax.axis_size("tp")
    count = lax.axis_size("ctx")
    tok = part * tp
    me = lax.axis_index("ctx").astype(jnp.int32)
    width = queries.shape[1] // tp
    step = width // CHUNKS

    kv = jnp.stack(
        (key_rows.reshape(part, tp, heads, DH), value_rows.reshape(part, tp, heads, DH)), axis=3
    )
    kv = kv.transpose(1, 2, 0, 3, 4).reshape(tp, heads, part, 2 * DH)
    kv = lax.all_to_all(kv, "tp", split_axis=0, concat_axis=0)
    q_parts = queries.reshape(part, tp, CHUNKS, step).transpose(2, 1, 0, 3)
    q_send = [q_parts[c] for c in range(CHUNKS)]
    kv, q_send = lax.optimization_barrier((kv, q_send))
    q_got = []
    for c in range(CHUNKS):
        got = lax.all_to_all(q_send[c], "tp", split_axis=0, concat_axis=0)
        if c + 1 < CHUNKS:
            got, q_send[c + 1] = lax.optimization_barrier((got, q_send[c + 1]))
        q_got.append(got.reshape(tok, step))

    bits = max((count - 1).bit_length(), 1)
    orders = (
        list(range(bits - 1, 0, -1)) + [0],
        list(range(1, bits)) + [0],
    )
    tables = []
    for head in range(heads):
        full = gather_ctx(kv[:, head].reshape(tok, 2 * DH), orders[head % 2])
        vk, vv, marks = gather_vertical(me[None], vertical_keys[head], full, tok)
        tables.append((vk, vv, full, marks.reshape(tok * count // SUB, SUB)))

    attended = None
    for c in range(CHUNKS):
        head = c * heads // CHUNKS
        meta = jnp.concatenate((me[None], slash_offsets[head] // SUB))
        attended = attend(
            meta, q_got[c], vertical_keys[head][None], *tables[head], attended, c, bands, width
        )
    return attended


def solution(mesh):
    in_specs = (
        P(("ctx", "tp"), None),
        P(("ctx", "tp"), None),
        P(("ctx", "tp"), None),
        P("tp", None),
        P("tp", None),
    )
    out_specs = P("ctx", "tp")
    return jax.shard_map(shards, mesh=mesh, in_specs=in_specs, out_specs=out_specs, check_vma=False)
```

profile of v0, /device:TPU:0, one launch (start us, length us, event | category | flops | bytes accessed | tf_op | source)
XLA Modules:
  0.0 226.1 jit_solution(463134875837681030)
XLA Ops:
  0.0 1.2 copy.17
  1.2 1.2 copy.18
  2.5 1.1 pad_maximum_fusion.4
  3.6 6.3 %all-to-all-start = ((bf16[4,2,256,256]{2,3,1,0:T(8,128)(2,1)}), bf16[4,2,256,256]{2,3,1,0:T(8,128)(2,1)S(1)}, u32[]{:S(2)}, u32[]{:S(2)}) async-start(bf16[4,2,256,256]{2,3,1,0:T(8,128)(2,1)} %bitcast.5), calls=%async_computation | async-start | bytes 2097152 | tf_op jit(solution)/shard_map/all_to_all | solution.py:203
  9.9 7.8 %reshape.37 = bf16[256,4,4,512]{3,2,1,0:T(4,128)(2,1)} reshape(bf16[256,8192]{1,0:T(8,128)(2,1)} %param.5) | data formatting | bytes 8388608 | tf_op jit(solution)/shard_map/reshape | solution.py:204
  17.7 4.5 %copy.27 = bf16[256,4,4,512]{3,0,1,2:T(8,128)(2,1)S(1)} copy(bf16[256,4,4,512]{3,2,1,0:T(4,128)(2,1)} %reshape.37) | data formatting | bytes 8388608 | tf_op jit(solution)/shard_map/reshape | solution.py:204
  22.2 2.1 slice_bitcast_fusion
  24.4 11.3 %all-to-all-done = bf16[4,2,256,256]{2,3,1,0:T(8,128)(2,1)S(1)} async-done(((bf16[4,2,256,256]{2,3,1,0:T(8,128)(2,1)}), bf16[4,2,256,256]{2,3,1,0:T(8,128)(2,1)S(1)}, u32[]{:S(2)}, u32[]{:S(2)}) %all-to-all-start) | async-done | bytes 1048608 | tf_op jit(solution)/shard_map/all_to_all | solution.py:203
  35.6 0.1 fusion
  35.7 0.2 copy.23
  35.9 1.6 collective-permute-start.3
  37.5 11.4 %collective-permute-done.3 = bf16[1,1024,256]{2,1,0:T(8,128)(2,1)S(1)} collective-permute-done((bf16[1,1024,256]{2,1,0:T(8,128)(2,1)S(1)}, bf16[1,1024,256]{2,1,0:T(8,128)(2,1)S(1)}, u32[]{:S(2)}, u32[]{:S(2)}) %collective-permute-start.3) | collective-permute-done | bytes 524320 | tf_op jit(solution)/shard_map/ppermute | solution.py:179
  48.9 1.1 pad_maximum_fusion.6
  50.0 1.5 collective-permute-start.4
  51.4 4.2 %all-to-all-start.1 = ((bf16[4,256,512]{2,1,0:T(8,128)(2,1)}), bf16[4,256,512]{2,1,0:T(8,128)(2,1)}, u32[]{:S(2)}, u32[]{:S(2)}) async-start(bf16[4,256,512]{2,1,0:T(8,128)(2,1)} %get-tuple-element.22), calls=%async_computation.1 | async-start | bytes 2097152 | tf_op jit(solution)/shard_map/all_to_all | solution.py:209
  55.7 0.2 copy.20
  55.9 0.6 collective-permute-start
  56.5 28.1 %collective-permute-done = bf16[1,1024,256]{2,1,0:T(8,128)(2,1)S(1)} collective-permute-done((bf16[1,1024,256]{2,1,0:T(8,128)(2,1)S(1)}, bf16[1,1024,256]{2,1,0:T(8,128)(2,1)S(1)}, u32[]{:S(2)}, u32[]{:S(2)}) %collective-permute-start) | collective-permute-done | bytes 524320 | tf_op jit(solution)/shard_map/ppermute | solution.py:179
  84.6 1.1 pad_maximum_fusion.5
  85.7 1.5 collective-permute-start.1
  87.2 1.5 pad_maximum_fusion.3
  88.7 4.4 %all-to-all-start.2 = ((bf16[4,256,512]{2,1,0:T(8,128)(2,1)}), bf16[4,256,512]{2,1,0:T(8,128)(2,1)}, u32[]{:S(2)}, u32[]{:S(2)}) async-start(bf16[4,256,512]{2,1,0:T(8,128)(2,1)} %get-tuple-element.24), calls=%async_computation.2 | async-start | bytes 2097152 | tf_op jit(solution)/shard_map/all_to_all | solution.py:209
  93.1 15.2 %collective-permute-done.1 = bf16[2,1024,256]{2,1,0:T(8,128)(2,1)} collective-permute-done((bf16[2,1024,256]{2,1,0:T(8,128)(2,1)}, bf16[2,1024,256]{2,1,0:T(8,128)(2,1)}, u32[]{:S(2)}, u32[]{:S(2)}) %collective-permute-start.1) | collective-permute-done | bytes 1048608 | tf_op jit(solution)/shard_map/ppermute | solution.py:179
  108.3 2.7 %pad_maximum_fusion.2 = bf16[4,1024,256]{2,1,0:T(8,128)(2,1)} fusion(bf16[2,1024,256]{2,1,0:T(8,128)(2,1)} %collective-permute-done.1, bf16[1,1024,256]{2,1,0:T(8,128)(2,1)S(1)} %collective-permute-done, bf16[1,1024,256]{2,1,0:T(8,128)(2,1)S(1)} %bitcast.62), kind=kLoop, calls=%fused_computation.3 | loop fusion | flops 2097152 | bytes 4194304 | tf_op jit(solution)/shard_map/concatenate | solution.py:179
  111.0 0.0 collective-permute-start.2
  111.0 0.6 slice_bitcast_fusion.4
  111.6 1.0 copy.25.column_ref
  112.7 1.0 copy.22.column_ref
  113.7 0.6 pad_add_fusion.1.meta_ref
  114.3 0.6 pad_add_fusion.meta_ref
  115.0 4.8 %all-to-all-done.2 = bf16[4,256,512]{2,1,0:T(8,128)(2,1)} async-done(((bf16[4,256,512]{2,1,0:T(8,128)(2,1)}), bf16[4,256,512]{2,1,0:T(8,128)(2,1)}, u32[]{:S(2)}, u32[]{:S(2)}) %all-to-all-start.2) | async-done | bytes 1048608 | tf_op jit(solution)/shard_map/all_to_all | solution.py:209
  119.7 4.3 %all-to-all-start.3 = ((bf16[4,256,512]{2,1,0:T(8,128)(2,1)}), bf16[4,256,512]{2,1,0:T(8,128)(2,1)}, u32[]{:S(2)}, u32[]{:S(2)}) async-start(bf16[4,256,512]{2,1,0:T(8,128)(2,1)} %get-tuple-element.26), calls=%async_computation.3 | async-start | bytes 2097152 | tf_op jit(solution)/shard_map/all_to_all | solution.py:209
  124.0 0.0 collective-permute-done.5
  124.0 1.8 pad_maximum_fusion.1
  125.8 2.3 %copy.24 = bf16[2,2,2,1024,256]{4,3,2,1,0:T(8,128)(2,1)} copy(bf16[2,2,2,1024,256]{4,3,0,1,2:T(8,128)(2,1)S(1)} %bitcast.54) | data formatting | bytes 8388608 | tf_op jit(solution)/shard_map/transpose | solution.py:184
  128.1 9.1 %gather_vertical.3 = (bf16[1024,128]{1,0:T(8,128)(2,1)}, bf16[1024,256]{1,0:T(8,128)(2,1)}, f32[16,512]{1,0:T(8,128)}) custom-call(s32[1]{0:T(128)} %bitcast.me_ref, s32[1024]{0:T(1024)} %bitcast.74, s32[1024,1]{1,0:T(8,128)} %copy.25.column_ref, bf16[8192,256]{1,0:T(8,128)(2,1)} %bitcast.64), custom_call_target="tpu_custom_call" | custom-call | flops 8589934592 | bytes 8388608 | tf_op jit(solution)/shard_map/gather_vertical/pallas_call | solution.py:52
  137.2 1.4 reshape.46.marks_ref
  138.6 2.1 pad_maximum_fusion
  140.7 2.3 copy.21
  143.0 9.0 %gather_vertical.2 = (bf16[1024,128]{1,0:T(8,128)(2,1)}, bf16[1024,256]{1,0:T(8,128)(2,1)}, f32[16,512]{1,0:T(8,128)}) custom-call(s32[1]{0:T(128)} %bitcast.me_ref, s32[1024]{0:T(1024)} %bitcast.73, s32[1024,1]{1,0:T(8,128)} %copy.22.column_ref, bf16[8192,256]{1,0:T(8,128)(2,1)} %bitcast.67), custom_call_target="tpu_custom_call" | custom-call | flops 8589934592 | bytes 8388608 | tf_op jit(solution)/shard_map/gather_vertical/pallas_call | solution.py:52
  152.0 1.5 reshape.41.marks_ref
  153.4 16.7 %attend_0.1.rest_0_ = bf16[1024,2048]{1,0:T(8,128)(2,1)} custom-call(s32[4]{0:T(128)} %pad_add_fusion.1.meta_ref, bf16[1024,512]{1,0:T(8,128)(2,1)} %bitcast.27.q_ref, s32[1,1024]{1,0:T(1,128)} %get-tuple-element.47.row_ref, bf16[1024,128]{1,0:T(8,128)(2,1)} %get-tuple-element.35.vk_ref, bf16[1024,256]{1,0:T(8,128)(2,1)} %get-tuple-element.36.vv_ref, ...), custom_call_target="tpu_custom_call" | custom-call | flops 9663676416 | bytes 8388608 | tf_op jit(solution)/shard_map/attend_0/pallas_call | solution.py:156
  170.1 0.0 all-to-all-done.3
  170.1 4.8 %all-to-all-start.4 = ((bf16[4,256,512]{2,1,0:T(8,128)(2,1)}), bf16[4,256,512]{2,1,0:T(8,128)(2,1)S(1)}, u32[]{:S(2)}, u32[]{:S(2)}) async-start(bf16[4,256,512]{2,1,0:T(8,128)(2,1)} %get-tuple-element.28), calls=%async_computation.4 | async-start | bytes 2097152 | tf_op jit(solution)/shard_map/all_to_all | solution.py:209
  174.9 16.7 %attend_1.1.rest_0_ = bf16[1024,2048]{1,0:T(8,128)(2,1)} custom-call(s32[4]{0:T(128)} %pad_add_fusion.1.meta_ref, bf16[1024,512]{1,0:T(8,128)(2,1)} %bitcast.20.q_ref, s32[1,1024]{1,0:T(1,128)} %get-tuple-element.47.row_ref, bf16[1024,128]{1,0:T(8,128)(2,1)} %get-tuple-element.35.vk_ref, ...), custom_call_target="tpu_custom_call", output_to_operand_aliasing={{}: (7, {})} | custom-call | flops 9663676416 | bytes 8388608 | tf_op jit(solution)/shard_map/attend_1/pallas_call | solution.py:156
  191.7 16.7 %attend_2.1.rest_0_ = bf16[1024,2048]{1,0:T(8,128)(2,1)} custom-call(s32[4]{0:T(128)} %pad_add_fusion.meta_ref, bf16[1024,512]{1,0:T(8,128)(2,1)} %bitcast.18.q_ref, s32[1,1024]{1,0:T(1,128)} %get-tuple-element.48.row_ref, bf16[1024,128]{1,0:T(8,128)(2,1)} %get-tuple-element.30.vk_ref, ...), custom_call_target="tpu_custom_call", output_to_operand_aliasing={{}: (7, {})} | custom-call | flops 9663676416 | bytes 8388608 | tf_op jit(solution)/shard_map/attend_2/pallas_call | solution.py:156
  208.4 1.0 copy-done
  209.4 16.7 %attend_3.1 = bf16[1024,2048]{1,0:T(8,128)(2,1)} custom-call(s32[4]{0:T(128)} %pad_add_fusion.meta_ref, bf16[1024,512]{1,0:T(8,128)(2,1)} %bitcast.72, s32[1,1024]{1,0:T(1,128)} %get-tuple-element.48.row_ref, bf16[1024,128]{1,0:T(8,128)(2,1)} %get-tuple-element.30.vk_ref, ...), custom_call_target="tpu_custom_call", output_to_operand_aliasing={{}: (7, {})} | custom-call | flops 9663676416 | bytes 8388608 | tf_op jit(solution)/shard_map/attend_3/pallas_call | solution.py:156
  (11 shorter events, 0.0 us)
Async XLA Ops:
  3.6 32.0 %all-to-all-start = ((bf16[4,2,256,256]{2,3,1,0:T(8,128)(2,1)}), bf16[4,2,256,256]{2,3,1,0:T(8,128)(2,1)S(1)}, u32[]{:S(2)}, u32[]{:S(2)}) async-start(bf16[4,2,256,256]{2,3,1,0:T(8,128)(2,1)} %bitcast.5), calls=%async_computation | async-start | bytes 2097152 | tf_op jit(solution)/shard_map/all_to_all | solution.py:203
  35.9 13.0 %collective-permute-start.3 = (bf16[1,1024,256]{2,1,0:T(8,128)(2,1)S(1)}, bf16[1,1024,256]{2,1,0:T(8,128)(2,1)S(1)}, u32[]{:S(2)}, u32[]{:S(2)}) collective-permute-start(bf16[1,1024,256]{2,1,0:T(8,128)(2,1)S(1)} %bitcast.56), channel_id=1, source_target_pairs={{0,16},{4,20},{8,24},{12,28},{16,0},{20,4},{24,8},{28,12},{1,17},{... | collective-permute-start | bytes 1572872 | tf_op jit(solution)/shard_map/ppermute | solution.py:179
  50.0 37.3 %collective-permute-start.4 = (bf16[2,1024,256]{2,1,0:T(8,128)(2,1)}, bf16[2,1024,256]{2,1,0:T(8,128)(2,1)S(1)}, u32[]{:S(2)}, u32[]{:S(2)}) collective-permute-start(bf16[2,1024,256]{2,1,0:T(8,128)(2,1)} %pad_maximum_fusion.6), channel_id=1, source_target_pairs={{0,8},{4,12},{8,0},{12,4},{16,24},{20,28},{24,16},{28,20},{1,9},{5... | collective-permute-start | bytes 3145736 | tf_op jit(solution)/shard_map/ppermute | solution.py:179
  51.4 37.3 %all-to-all-start.1 = ((bf16[4,256,512]{2,1,0:T(8,128)(2,1)}), bf16[4,256,512]{2,1,0:T(8,128)(2,1)}, u32[]{:S(2)}, u32[]{:S(2)}) async-start(bf16[4,256,512]{2,1,0:T(8,128)(2,1)} %get-tuple-element.22), calls=%async_computation.1 | async-start | bytes 2097152 | tf_op jit(solution)/shard_map/all_to_all | solution.py:209
  55.9 28.7 %collective-permute-start = (bf16[1,1024,256]{2,1,0:T(8,128)(2,1)S(1)}, bf16[1,1024,256]{2,1,0:T(8,128)(2,1)S(1)}, u32[]{:S(2)}, u32[]{:S(2)}) collective-permute-start(bf16[1,1024,256]{2,1,0:T(8,128)(2,1)S(1)} %bitcast.60), channel_id=1, source_target_pairs={{0,8},{4,12},{8,0},{12,4},{16,24},{20,28},{24,16},{28,20},{1,9},{5... | collective-permute-start | bytes 1572872 | tf_op jit(solution)/shard_map/ppermute | solution.py:179
  85.7 22.6 %collective-permute-start.1 = (bf16[2,1024,256]{2,1,0:T(8,128)(2,1)}, bf16[2,1024,256]{2,1,0:T(8,128)(2,1)}, u32[]{:S(2)}, u32[]{:S(2)}) collective-permute-start(bf16[2,1024,256]{2,1,0:T(8,128)(2,1)} %pad_maximum_fusion.5), channel_id=1, source_target_pairs={{0,16},{4,20},{8,24},{12,28},{16,0},{20,4},{24,8},{28,12},{1,17},{... | collective-permute-start | bytes 3145736 | tf_op jit(solution)/shard_map/ppermute | solution.py:179
  88.7 22.3 %copy-start.1 = (s32[2,1024]{1,0:T(2,128)S(1)}, s32[2,1024]{1,0:T(2,128)}, u32[]{:S(2)}) copy-start(s32[2,1024]{1,0:T(2,128)} %param.8) | copy-start | bytes 24580
  88.7 25.0 %copy-start.2 = (s32[2,3]{1,0:T(2,128)S(1)}, s32[2,3]{1,0:T(2,128)}, u32[]{:S(2)}) copy-start(s32[2,3]{1,0:T(2,128)} %param.9) | copy-start | bytes 76
  88.7 35.3 %collective-permute-start.5 = (bf16[4,1024,256]{2,1,0:T(8,128)(2,1)}, bf16[4,1024,256]{2,1,0:T(8,128)(2,1)}, u32[]{:S(2)}, u32[]{:S(2)}) collective-permute-start(bf16[4,1024,256]{2,1,0:T(8,128)(2,1)} %pad_maximum_fusion.3), channel_id=1, source_target_pairs={{0,4},{4,0},{8,12},{12,8},{16,20},{20,16},{24,28},{28,24},{1,5},{5... | collective-permute-start | bytes 6291464 | tf_op jit(solution)/shard_map/ppermute | solution.py:179
  88.7 31.0 %all-to-all-start.2 = ((bf16[4,256,512]{2,1,0:T(8,128)(2,1)}), bf16[4,256,512]{2,1,0:T(8,128)(2,1)}, u32[]{:S(2)}, u32[]{:S(2)}) async-start(bf16[4,256,512]{2,1,0:T(8,128)(2,1)} %get-tuple-element.24), calls=%async_computation.2 | async-start | bytes 2097152 | tf_op jit(solution)/shard_map/all_to_all | solution.py:209
  111.0 27.6 %collective-permute-start.2 = (bf16[4,1024,256]{2,1,0:T(8,128)(2,1)}, bf16[4,1024,256]{2,1,0:T(8,128)(2,1)}, u32[]{:S(2)}, u32[]{:S(2)}) collective-permute-start(bf16[4,1024,256]{2,1,0:T(8,128)(2,1)} %pad_maximum_fusion.2), channel_id=1, source_target_pairs={{0,4},{4,0},{8,12},{12,8},{16,20},{20,16},{24,28},{28,24},{1,5},{5... | collective-permute-start | bytes 6291464 | tf_op jit(solution)/shard_map/ppermute | solution.py:179
  119.7 50.4 %all-to-all-start.3 = ((bf16[4,256,512]{2,1,0:T(8,128)(2,1)}), bf16[4,256,512]{2,1,0:T(8,128)(2,1)}, u32[]{:S(2)}, u32[]{:S(2)}) async-start(bf16[4,256,512]{2,1,0:T(8,128)(2,1)} %get-tuple-element.26), calls=%async_computation.3 | async-start | bytes 2097152 | tf_op jit(solution)/shard_map/all_to_all | solution.py:209
  170.1 38.2 %all-to-all-start.4 = ((bf16[4,256,512]{2,1,0:T(8,128)(2,1)}), bf16[4,256,512]{2,1,0:T(8,128)(2,1)S(1)}, u32[]{:S(2)}, u32[]{:S(2)}) async-start(bf16[4,256,512]{2,1,0:T(8,128)(2,1)} %get-tuple-element.28), calls=%async_computation.4 | async-start | bytes 2097152 | tf_op jit(solution)/shard_map/all_to_all | solution.py:209
  208.4 1.0 copy-start
where the time goes:
time: 227 us; the launch traced here: 226 us
  Pallas kernels  84.9 us (37%)
  waiting for transfers between devices  70.7 us (31%)
  starting transfers between devices  29.2 us (13%)
  local copies, waits for them, and re-layouts  28.5 us (13%)
  other arithmetic  12.6 us (6%)
    pallas_call x4, Pallas kernels, attend(): pl.pallas_call(functools.partial(attend_body, tok, bands, group), out_sha...  66.8 us
    ppermute x6, waiting for transfers between devices, gather_ctx(): held = jnp.concatenate((held, lax.ppermute(held, 'ctx', route)), axis=0)  54.6 us
    pallas_call x2, Pallas kernels, gather_vertical(): pl.pallas_call(functools.partial(gather_body, tok), out_shape=(jax.ShapeD...  18.1 us
    all_to_all x4, starting transfers between devices, shards(): got = lax.all_to_all(q_send[c], 'tp', split_axis=0, concat_axis=0)  17.7 us
    reshape x2, local copies, waits for them, and re-layouts, shards(): q_parts = queries.reshape(part, tp, CHUNKS, step).transpose(2, 1, 0, 3)  12.3 us
    all_to_all x1, waiting for transfers between devices, shards(): kv = lax.all_to_all(kv, 'tp', split_axis=0, concat_axis=0)  11.3 us
    concatenate x6, other arithmetic, gather_ctx(): held = jnp.concatenate((held, lax.ppermute(held, 'ctx', route)), axis=0)  10.3 us
    all_to_all x1, starting transfers between devices, shards(): kv = lax.all_to_all(kv, 'tp', split_axis=0, concat_axis=0)  6.32 us
  transfers between devices with their start and end apart: 11, of which 5 were waited for; matrix products, arithmetic and copies ran while one was open for 16% of the time, Pallas kernels for 30%

commit v1 on v0

v1 whole, which is shorter than its diff:
```python
import functools
import math

import jax
import jax.numpy as jnp
from jax import lax
from jax.experimental import pallas as pl
from jax.experimental.pallas import tpu as pltpu
from jax.sharding import PartitionSpec as P

HQ = 64
KVH = 8
DH = 128
SUB = 64
CHUNKS = 4
VT = 256
PB = 512
EXP2_SCALE = DH**-0.5 * math.log2(math.e)
MASKED = -1e30
VMEM_BYTES = 60 * 1024 * 1024
MESH = pl.DeviceIdType.MESH
F32 = jnp.float32
BF16 = jnp.bfloat16


def ctx_orders(bits, heads):
    far = list(range(bits - 1, 0, -1))
    return [(far if head % 2 == 0 else far[::-1]) + [0] for head in range(heads)]


def body(sizes, pick_ref, q_hbm, k_hbm, v_hbm, column_ref, row_ref, o_hbm, *scratch):
    tok, heads, bands, tp, count, group = sizes
    (kv, qs, outs, vert_sum, vk, vv, marks, joined, win, mark_win) = scratch[:10]
    (kv_loc, kv_snd, kv_rcv, q_loc, q_snd, q_rcv, c_snd, c_rcv, o_sem) = scratch[10:]
    part = tok // tp
    step = group * DH
    bits = max((count - 1).bit_length(), 1)
    me_c = lax.axis_index("ctx")
    me_t = lax.axis_index("tp")

    def across(bit):
        weight = 1 << bit
        return me_c + weight - 2 * weight * ((me_c // weight) % 2)

    ring = [lax.rem(me_t + k, tp) for k in range(tp)]
    peers = [(me_c, ring[k]) for k in range(1, tp)] + [(across(b), me_t) for b in range(bits)]
    barrier = pltpu.get_barrier_semaphore()
    for peer in peers:
        pl.semaphore_signal(barrier, inc=1, device_id=peer, device_id_type=MESH)
    pl.semaphore_wait(barrier, len(peers))

    own_rows = pl.ds(pl.multiple_of(me_t * part, part), part)

    def kv_copy(k, head, side):
        source = (k_hbm, v_hbm)[side]
        first = pl.multiple_of((ring[k] * heads + head) * DH, DH)
        source = source.at[:, pl.ds(first, DH)]
        target = kv.at[head, own_rows, pl.ds(side * DH, DH)]
        if k == 0:
            return pltpu.make_async_copy(source, target, kv_loc.at[head, side])
        return pltpu.make_async_remote_copy(
            src_ref=source,
            dst_ref=target,
            send_sem=kv_snd.at[k - 1, head, side],
            recv_sem=kv_rcv.at[k - 1, head, side],
            device_id=(me_c, ring[k]),
            device_id_type=MESH,
        )

    def q_copy(k, chunk):
        first = pl.multiple_of(ring[k] * (CHUNKS * step) + chunk * step, step)
        source = q_hbm.at[:, pl.ds(first, step)]
        target = qs.at[chunk, own_rows]
        if k == 0:
            return pltpu.make_async_copy(source, target, q_loc.at[chunk])
        return pltpu.make_async_remote_copy(
            src_ref=source,
            dst_ref=target,
            send_sem=q_snd.at[k - 1, chunk],
            recv_sem=q_rcv.at[k - 1, chunk],
            device_id=(me_c, ring[k]),
            device_id_type=MESH,
        )

    def ctx_copy(head, slot, bit):
        there = slot ^ (1 << bit)
        return pltpu.make_async_remote_copy(
            src_ref=kv.at[head, pl.ds(slot * tok, tok)],
            dst_ref=kv.at[head, pl.ds(there * tok, tok)],
            send_sem=c_snd.at[head, there],
            recv_sem=c_rcv.at[head, there],
            device_id=(across(bit), me_t),
            device_id_type=MESH,
        )

    sent = []

    def start_q(chunk):
        for k in range(tp - 1, 0, -1):
            copy = q_copy(k, chunk)
            copy.start()
            sent.append(copy)

    def add_vertical(head, slot):
        def one_block(index, carry):
            block = slot * (tok // PB) + index
            base = block * PB
            rows = kv[head, pl.ds(pl.multiple_of(base, PB), PB), :]
            lanes = lax.broadcasted_iota(jnp.int32, (VT, PB), 1) + base
            seen = jnp.zeros((1, PB), F32)
            for tile in range(vk.shape[1] // VT):
                span = pl.ds(tile * VT, VT)
                hit = jnp.where(column_ref[head, span, :] == lanes, 1.0, 0.0)
                seen += jnp.sum(hit, axis=0, keepdims=True)
                vert_sum[head, span, :] += jnp.dot(
                    hit.astype(BF16), rows, preferred_element_type=F32
                )
            for piece in range(PB // SUB):
                marks[head, pl.ds(block * (PB // SUB) + piece, 1), :] = seen[
                    :, piece * SUB : (piece + 1) * SUB
                ]
            return carry

        lax.fori_loop(0, tok // PB, one_block, 0)

    for head in range(heads):
        for side in range(2):
            for k in range(tp - 1, 0, -1):
                copy = kv_copy(k, head, side)
                copy.start()
                sent.append(copy)
            kv_copy(0, head, side).start()
    for chunk in range(CHUNKS):
        q_copy(0, chunk).start()
    vert_sum[...] = jnp.zeros_like(vert_sum)

    orders = ctx_orders(bits, heads)
    for head in range(heads):
        for side in range(2):
            kv_copy(0, head, side).wait()
            for k in range(1, tp):
                kv_copy(k, head, side).wait_recv()
        for bit in orders[head]:
            copy = ctx_copy(head, 0, bit)
            copy.start()
            sent.append(copy)
    start_q(0)
    for head in range(heads):
        add_vertical(head, 0)
    held = [[0] for _ in range(heads)]
    for turn in range(bits):
        fresh = [[slot ^ (1 << orders[head][turn]) for slot in held[head]] for head in range(heads)]
        for index in range(len(fresh[0])):
            for head in range(heads):
                ctx_copy(head, held[head][index], orders[head][turn]).wait_recv()
                for bit in orders[head][turn + 1 :]:
                    copy = ctx_copy(head, fresh[head][index], bit)
                    copy.start()
                    sent.append(copy)
        if turn < 2:
            start_q(1 + turn)
        for head in range(heads):
            for slot in fresh[head]:
                add_vertical(head, slot)
            held[head] += fresh[head]
    for chunk in range(1 + min(bits, 2), CHUNKS):
        start_q(chunk)

    for head in range(heads):
        vk[head] = vert_sum[head, :, :DH].astype(BF16)
        vv[head, :, :DH] = vert_sum[head, :, DH:].astype(BF16)
        vv[head, :, DH:] = jnp.ones((vv.shape[1], DH), BF16)

    per_dev = tok // SUB
    shifts = [1 << b for b in reversed(range(per_dev.bit_length() - 1))]

    def cut_window(head, band):
        entry = (head * bands + band) * (2 + len(shifts))
        picks = [pick_ref[entry + i] for i in range(2 + len(shifts))]

        def join(index, carry):
            piece = pl.multiple_of(index * SUB, SUB)
            both = [jnp.zeros((SUB, 2 * DH), BF16)] * 2
            for slot in range(count):
                rows = kv[head, pl.ds(slot * tok + piece, SUB), :]
                both = [lax.select(picks[i] == slot, rows, both[i]) for i in range(2)]
            for i in range(2):
                joined[pl.ds(i * tok + piece, SUB), :] = both[i]
            return carry

        lax.fori_loop(0, per_dev, join, 0)
        for turn, shift in enumerate(shifts):
            last = turn == len(shifts) - 1

            def move(index, carry):
                here = pl.ds(pl.multiple_of(index * SUB, SUB), SUB)
                there = pl.ds(pl.multiple_of((index + shift) * SUB, SUB), SUB)
                rows = lax.select(picks[2 + turn] == 1, joined[there, :], joined[here, :])
                if last:
                    win[head, band, here, :] = rows
                else:
                    joined[here, :] = rows
                return carry

            lax.fori_loop(0, per_dev + shift, move, 0)
        both = [jnp.ones((per_dev, SUB), F32)] * 2
        for slot in range(count):
            rows = marks[head, slot * per_dev : (slot + 1) * per_dev, :]
            both = [lax.select(picks[i] == slot, rows, both[i]) for i in range(2)]
        both = jnp.concatenate(both, axis=0)
        for turn, shift in enumerate(shifts):
            moved = jnp.concatenate((both[shift:], both[:shift]), axis=0)
            both = lax.select(picks[2 + turn] == 1, moved, both)
        mark_win[head, band] = both

    for head in range(heads):
        for band in range(bands):
            cut_window(head, band)

    rows = group * SUB
    slots = 4 * SUB
    nt = (((1,), (1,)), ((), ()))

    def attend(chunk, head, sub):
        upper = (
            lax.broadcasted_iota(jnp.int32, (rows, slots), 1) % SUB
            > lax.broadcasted_iota(jnp.int32, (rows, slots), 0) % SUB
        )
        ones = jnp.ones((slots, DH), BF16)
        sides = []
        for back in (1, 0):
            blocks, biases = [], []
            for band in range(bands):
                first = pl.multiple_of((sub + 1 - back) * SUB, SUB)
                blocks.append(win[head, band, pl.ds(first, SUB), :])
                if band == 0 and back == 0:
                    biases.append(jnp.zeros((1, SUB), F32))
                else:
                    gone = mark_win[head, band, pl.ds(sub + 1 - back, 1), :]
                    biases.append(jnp.where(gone > 0.5, MASKED, 0.0))
            for _ in range(4 - bands):
                blocks.append(jnp.zeros((SUB, 2 * DH), BF16))
                biases.append(jnp.full((1, SUB), MASKED, F32))
            sides.append((jnp.concatenate(blocks, axis=0), jnp.concatenate(biases, axis=1)))
        (near, near_bias), (own, own_bias) = sides
        here = pl.ds(pl.multiple_of(sub * SUB, SUB), SUB)
        q = jnp.concatenate(
            [qs[chunk, here, g * DH : (g + 1) * DH] for g in range(group)], axis=0
        )
        vert_bias = jnp.where(row_ref[head] < me_c * tok + sub * SUB, 0.0, MASKED)
        vert = lax.dot_general(q, vk[head], nt, preferred_element_type=F32) + vert_bias
        s_near = lax.dot_general(q, near[:, :DH], nt, preferred_element_type=F32)
        s_own = lax.dot_general(q, own[:, :DH], nt, preferred_element_type=F32)
        band = jnp.where(upper, s_near + near_bias, s_own + own_bias)
        top = jnp.maximum(
            jnp.max(vert, axis=1, keepdims=True), jnp.max(band, axis=1, keepdims=True)
        )
        p_vert = jnp.exp2((vert - top) * EXP2_SCALE).astype(BF16)
        p_band = jnp.exp2((band - top) * EXP2_SCALE)
        p_near = jnp.where(upper, p_band, 0.0).astype(BF16)
        p_own = jnp.where(upper, 0.0, p_band).astype(BF16)
        near_v = jnp.concatenate((near[:, DH:], ones), axis=1)
        own_v = jnp.concatenate((own[:, DH:], ones), axis=1)
        acc = jnp.dot(p_vert, vv[head], preferred_element_type=F32)
        acc += jnp.dot(p_near, near_v, preferred_element_type=F32)
        acc += jnp.dot(p_own, own_v, preferred_element_type=F32)
        out = (acc[:, :DH] / acc[:, DH:]).astype(BF16)
        for g in range(group):
            outs[chunk, here, g * DH : (g + 1) * DH] = out[g * SUB : (g + 1) * SUB]

    def out_copy(chunk):
        return pltpu.make_async_copy(
            outs.at[chunk], o_hbm.at[:, pl.ds(chunk * step, step)], o_sem.at[chunk]
        )

    for chunk in range(CHUNKS):
        q_copy(0, chunk).wait()
        for k in range(1, tp):
            q_copy(k, chunk).wait_recv()
        head = chunk * heads // CHUNKS

        def pair(index, carry):
            attend(chunk, head, index * 2)
            attend(chunk, head, index * 2 + 1)
            return carry

        lax.fori_loop(0, tok // SUB // 2, pair, 0)
        out_copy(chunk).start()
    for chunk in range(CHUNKS):
        out_copy(chunk).wait()
    for copy in sent:
        copy.wait_send()


def shards(queries, key_rows, value_rows, vertical_keys, slash_offsets):
    heads, vert_count = vertical_keys.shape
    bands = slash_offsets.shape[1]
    part = queries.shape[0]
    tp = lax.axis_size("tp")
    count = lax.axis_size("ctx")
    tok = part * tp
    total = tok * count
    me = lax.axis_index("ctx").astype(jnp.int32)
    width = queries.shape[1] // tp
    step = width // CHUNKS

    per_dev = tok // SUB
    start = me * per_dev - slash_offsets // SUB - 1
    low = start // per_dev
    rest = start % per_dev
    picks = [jnp.where(low + i >= 0, (low + i) ^ me, -1) for i in range(2)]
    picks += [(rest >> b) & 1 for b in reversed(range(per_dev.bit_length() - 1))]
    picks = jnp.stack(picks, axis=2).reshape(-1)
    column = (((vertical_keys // tok) ^ me) * tok + vertical_keys % tok)[:, :, None]

    vmem = pl.BlockSpec(memory_space=pltpu.VMEM)
    smem = pl.BlockSpec(memory_space=pltpu.SMEM)
    hbm = pl.BlockSpec(memory_space=pl.ANY)
    dma = pltpu.SemaphoreType.DMA
    scores = tok * (width // DH) * 1536
    return pl.pallas_call(
        functools.partial(body, (tok, heads, bands, tp, count, step // DH)),
        out_shape=jax.ShapeDtypeStruct((tok, width), BF16),
        in_specs=[smem, hbm, hbm, hbm, vmem, vmem],
        out_specs=hbm,
        scratch_shapes=[
            pltpu.VMEM((heads, total, 2 * DH), BF16),
            pltpu.VMEM((CHUNKS, tok, step), BF16),
            pltpu.VMEM((CHUNKS, tok, step), BF16),
            pltpu.VMEM((heads, vert_count, 2 * DH), F32),
            pltpu.VMEM((heads, vert_count, DH), BF16),
            pltpu.VMEM((heads, vert_count, 2 * DH), BF16),
            pltpu.VMEM((heads, total // SUB, SUB), F32),
            pltpu.VMEM((2 * tok, 2 * DH), BF16),
            pltpu.VMEM((heads, bands, tok + SUB, 2 * DH), BF16),
            pltpu.VMEM((heads, bands, 2 * tok // SUB, SUB), F32),
            dma((heads, 2)),
            dma((tp - 1, heads, 2)),
            dma((tp - 1, heads, 2)),
            dma((CHUNKS,)),
            dma((tp - 1, CHUNKS)),
            dma((tp - 1, CHUNKS)),
            dma((heads, count)),
            dma((heads, count)),
            dma((CHUNKS,)),
        ],
        compiler_params=pltpu.CompilerParams(
            collective_id=0, has_side_effects=True, vmem_limit_bytes=VMEM_BYTES
        ),
        cost_estimate=pl.CostEstimate(
            flops=scores * 1024, bytes_accessed=32 << 20, transcendentals=scores
        ),
        name="attend_all",
    )(picks, queries, key_rows, value_rows, column, vertical_keys[:, None, :])


def solution(mesh):
    in_specs = (
        P(("ctx", "tp"), None),
        P(("ctx", "tp"), None),
        P(("ctx", "tp"), None),
        P("tp", None),
        P("tp", None),
    )
    out_specs = P("ctx", "tp")
    return jax.shard_map(shards, mesh=mesh, in_specs=in_specs, out_specs=out_specs, check_vma=False)
```

time: 227 us -> 151 us (0.67)
  waiting for transfers between devices: 70.7 us -> 0 us
  Pallas kernels: 84.9 us -> 141 us
  starting transfers between devices: 29.2 us -> 0 us
  local copies, waits for them, and re-layouts: 28.5 us -> 8.21 us
  other arithmetic: 12.6 us -> 1.52 us
    pallas_call x6 -> x1, Pallas kernels: 84.9 us -> 141 us  [shards(): pl.pallas_call(functools.partial(body, (tok, heads, bands, tp, count, ste...]
    ppermute x6 -> x0, waiting for transfers between devices: 54.6 us -> none  [gather_ctx(): held = jnp.concatenate((held, lax.ppermute(held, 'ctx', route)), axis=0)]
    all_to_all x5 -> x0, starting transfers between devices: 24 us -> none  [the longest x4 17.7 us: shards(): got = lax.all_to_all(q_send[c], 'tp', split_axis=0, concat_axis=0)]
    all_to_all x5 -> x0, waiting for transfers between devices: 16 us -> none  [the longest x1 11.3 us: shards(): kv = lax.all_to_all(kv, 'tp', split_axis=0, concat_axis=0)]
    reshape x4 -> x1, local copies, waits for them, and re-layouts: 15.2 us -> 0.68 us  [shards(): picks = jnp.stack(picks, axis=2).reshape(-1)]
    concatenate x8 -> x0, other arithmetic: 11.5 us -> none  [the longest x6 10.3 us: gather_ctx(): held = jnp.concatenate((held, lax.ppermute(held, 'ctx', route)), axis=0)]
    ppermute x6 -> x0, starting transfers between devices: 5.2 us -> none  [gather_ctx(): held = jnp.concatenate((held, lax.ppermute(held, 'ctx', route)), axis=0)]
    transpose x2 -> x0, local copies, waits for them, and re-layouts: 4.55 us -> none  [gather_ctx(): held = held.transpose(axes + [bits, bits + 1])]
  transfers between devices with their start and end apart: 11 -> 0, of which waited for: 5 -> 0; matrix products, arithmetic and copies ran while one was open for 16% -> 0% of each run, Pallas kernels for 30% -> 0%
where the time goes in v1:
time: 151 us
  Pallas kernels  141 us (93%)
  local copies, waits for them, and re-layouts  8.21 us (5%)
  other arithmetic  1.52 us (1%)
    pallas_call x1, Pallas kernels, shards(): pl.pallas_call(functools.partial(body, (tok, heads, bands, tp, count, ste...  141 us
    unnamed x1, local copies, waits for them, and re-layouts  4.79 us

profile of v1, /device:TPU:0, one launch (start us, length us, event | category | flops | bytes accessed | tf_op | source)
XLA Modules:
  0.0 150.8 jit_solution(15457563611297336108)
XLA Ops:
  0.0 0.7 constant_dynamic-update-slice_fusion.5
  0.8 0.1 copy.7
  0.9 0.7 reshape.3.pick_ref
  1.6 0.7 fusion.1
  2.3 1.3 broadcast_in_dim.10.row_ref
  3.6 1.3 copy.8.column_ref
  4.9 141.0 %attend_all.1 = bf16[1024,2048]{1,0:T(8,128)(2,1)} custom-call(s32[36]{0:T(128)} %reshape.3.pick_ref, bf16[256,8192]{1,0:T(8,128)(2,1)} %q_hbm.1, bf16[256,1024]{1,0:T(8,128)(2,1)} %k_hbm.1, bf16[256,1024]{1,0:T(8,128)(2,1)} %v_hbm.1, s32[2,1024,1]{2,1,0:T(8,128)} %copy.8.column_ref, s32[2,1,1024]{2,1,0:T(1,128)} %broadcast_in_dim.10.row_ref), custom_call_target="tpu_custom_call" | custom-call | flops 25769803776 | bytes 33554432 | tf_op jit(solution)/shard_map/attend_all/pallas_call | solution.py:321
  146.0 4.8 %copy.15 = bf16[1024,2048]{1,0:T(8,128)(2,1)} copy(bf16[1024,2048]{1,0:T(8,128)(2,1)} %attend_all.1) | data formatting | bytes 8388608
  (5 shorter events, 0.1 us)

commit v2 on v1

--- a/solution.py
+++ b/solution.py
@@ -12,7 +12,7 @@
 KVH = 8
 DH = 128
 SUB = 64
-CHUNKS = 4
+HALVES = 2
 VT = 256
 PB = 512
 EXP2_SCALE = DH**-0.5 * math.log2(math.e)
@@ -34,6 +34,8 @@
     (kv_loc, kv_snd, kv_rcv, q_loc, q_snd, q_rcv, c_snd, c_rcv, o_sem) = scratch[10:]
     part = tok // tp
     step = group * DH
+    share = part // HALVES
+    chunks = heads * HALVES
     bits = max((count - 1).bit_length(), 1)
     me_c = lax.axis_index("ctx")
     me_t = lax.axis_index("tp")
@@ -68,9 +70,11 @@
         )
 
     def q_copy(k, chunk):
-        first = pl.multiple_of(ring[k] * (CHUNKS * step) + chunk * step, step)
-        source = q_hbm.at[:, pl.ds(first, step)]
-        target = qs.at[chunk, own_rows]
+        head, half = chunk // HALVES, chunk % HALVES
+        first = pl.multiple_of((ring[k] * heads + head) * step, step)
+        source = q_hbm.at[pl.ds(half * share, share), pl.ds(first, step)]
+        landing = pl.multiple_of(me_t * part + half * share, share)
+        target = qs.at[head, pl.ds(landing, share)]
         if k == 0:
             return pltpu.make_async_copy(source, target, q_loc.at[chunk])
         return pltpu.make_async_remote_copy(
@@ -82,13 +86,14 @@
             device_id_type=MESH,
         )
 
-    def ctx_copy(head, slot, bit):
+    def ctx_copy(head, slot, bit, k):
         there = slot ^ (1 << bit)
+        quarter = lax.rem(me_t - k + tp, tp) * part
         return pltpu.make_async_remote_copy(
-            src_ref=kv.at[head, pl.ds(slot * tok, tok)],
-            dst_ref=kv.at[head, pl.ds(there * tok, tok)],
-            send_sem=c_snd.at[head, there],
-            recv_sem=c_rcv.at[head, there],
+            src_ref=kv.at[head, pl.ds(pl.multiple_of(slot * tok + quarter, part), part)],
+            dst_ref=kv.at[head, pl.ds(pl.multiple_of(there * tok + quarter, part), part)],
+            send_sem=c_snd.at[head, there, k],
+            recv_sem=c_rcv.at[head, there, k],
             device_id=(across(bit), me_t),
             device_id_type=MESH,
         )
@@ -123,27 +128,29 @@
 
         lax.fori_loop(0, tok // PB, one_block, 0)
 
-    for head in range(heads):
-        for side in range(2):
-            for k in range(tp - 1, 0, -1):
+    for k in range(tp):
+        for head in range(heads):
+            for side in range(2):
                 copy = kv_copy(k, head, side)
                 copy.start()
-                sent.append(copy)
-            kv_copy(0, head, side).start()
-    for chunk in range(CHUNKS):
+                if k > 0:
+                    sent.append(copy)
+    for chunk in range(chunks):
         q_copy(0, chunk).start()
     vert_sum[...] = jnp.zeros_like(vert_sum)
 
     orders = ctx_orders(bits, heads)
-    for head in range(heads):
-        for side in range(2):
-            kv_copy(0, head, side).wait()
-            for k in range(1, tp):
-                kv_copy(k, head, side).wait_recv()
-        for bit in orders[head]:
-            copy = ctx_copy(head, 0, bit)
-            copy.start()
-            sent.append(copy)
+    for k in range(tp):
+        for head in range(heads):
+            for side in range(2):
+                if k == 0:
+                    kv_copy(k, head, side).wait()
+                else:
+                    kv_copy(k, head, side).wait_recv()
+            for bit in orders[head]:
+                copy = ctx_copy(head, 0, bit, k)
+                copy.start()
+                sent.append(copy)
     start_q(0)
     for head in range(heads):
         add_vertical(head, 0)
@@ -151,19 +158,20 @@
     for turn in range(bits):
         fresh = [[slot ^ (1 << orders[head][turn]) for slot in held[head]] for head in range(heads)]
         for index in range(len(fresh[0])):
-            for head in range(heads):
-                ctx_copy(head, held[head][index], orders[head][turn]).wait_recv()
-                for bit in orders[head][turn + 1 :]:
-                    copy = ctx_copy(head, fresh[head][index], bit)
-                    copy.start()
-                    sent.append(copy)
+            for k in range(tp):
+                for head in range(heads):
+                    ctx_copy(head, held[head][index], orders[head][turn], k).wait_recv()
+                    for bit in orders[head][turn + 1 :]:
+                        copy = ctx_copy(head, fresh[head][index], bit, k)
+                        copy.start()
+                        sent.append(copy)
         if turn < 2:
             start_q(1 + turn)
         for head in range(heads):
             for slot in fresh[head]:
                 add_vertical(head, slot)
             held[head] += fresh[head]
-    for chunk in range(1 + min(bits, 2), CHUNKS):
+    for chunk in range(1 + min(bits, 2), chunks):
         start_q(chunk)
 
     for head in range(heads):
@@ -221,7 +229,7 @@
     slots = 4 * SUB
     nt = (((1,), (1,)), ((), ()))
 
-    def attend(chunk, head, sub):
+    def scores(head, sub):
         upper = (
             lax.broadcasted_iota(jnp.int32, (rows, slots), 1) % SUB
             > lax.broadcasted_iota(jnp.int32, (rows, slots), 0) % SUB
@@ -245,13 +253,18 @@
         (near, near_bias), (own, own_bias) = sides
         here = pl.ds(pl.multiple_of(sub * SUB, SUB), SUB)
         q = jnp.concatenate(
-            [qs[chunk, here, g * DH : (g + 1) * DH] for g in range(group)], axis=0
-        )
-        vert_bias = jnp.where(row_ref[head] < me_c * tok + sub * SUB, 0.0, MASKED)
+            [qs[head, here, g * DH : (g + 1) * DH] for g in range(group)], axis=0
+        )
+        vert_bias = jnp.where(row_ref[head : head + 1, :] < me_c * tok + sub * SUB, 0.0, MASKED)
         vert = lax.dot_general(q, vk[head], nt, preferred_element_type=F32) + vert_bias
         s_near = lax.dot_general(q, near[:, :DH], nt, preferred_element_type=F32)
         s_own = lax.dot_general(q, own[:, :DH], nt, preferred_element_type=F32)
         band = jnp.where(upper, s_near + near_bias, s_own + own_bias)
+        near_v = jnp.concatenate((near[:, DH:], ones), axis=1)
+        own_v = jnp.concatenate((own[:, DH:], ones), axis=1)
+        return vert, band, upper, near_v, own_v
+
+    def finish(head, sub, vert, band, upper, near_v, own_v):
         top = jnp.maximum(
             jnp.max(vert, axis=1, keepdims=True), jnp.max(band, axis=1, keepdims=True)
         )
@@ -259,35 +272,41 @@
         p_band = jnp.exp2((band - top) * EXP2_SCALE)
         p_near = jnp.where(upper, p_band, 0.0).astype(BF16)
         p_own = jnp.where(upper, 0.0, p_band).astype(BF16)
-        near_v = jnp.concatenate((near[:, DH:], ones), axis=1)
-        own_v = jnp.concatenate((own[:, DH:], ones), axis=1)
         acc = jnp.dot(p_vert, vv[head], preferred_element_type=F32)
         acc += jnp.dot(p_near, near_v, preferred_element_type=F32)
         acc += jnp.dot(p_own, own_v, preferred_element_type=F32)
         out = (acc[:, :DH] / acc[:, DH:]).astype(BF16)
+        here = pl.ds(pl.multiple_of(sub * SUB, SUB), SUB)
         for g in range(group):
-            outs[chunk, here, g * DH : (g + 1) * DH] = out[g * SUB : (g + 1) * SUB]
-
-    def out_copy(chunk):
+            outs[head, here, g * DH : (g + 1) * DH] = out[g * SUB : (g + 1) * SUB]
+
+    def out_copy(head, half, source):
+        here = pl.ds(pl.multiple_of(source * part + half * share, share), share)
         return pltpu.make_async_copy(
-            outs.at[chunk], o_hbm.at[:, pl.ds(chunk * step, step)], o_sem.at[chunk]
-        )
-
-    for chunk in range(CHUNKS):
+            outs.at[head, here],
+            o_hbm.at[here, pl.ds(head * step, step)],
+            o_sem.at[head * HALVES + half, source],
+        )
+
+    for chunk in range(chunks):
         q_copy(0, chunk).wait()
         for k in range(1, tp):
             q_copy(k, chunk).wait_recv()
-        head = chunk * heads // CHUNKS
-
-        def pair(index, carry):
-            attend(chunk, head, index * 2)
-            attend(chunk, head, index * 2 + 1)
+        head, half = chunk // HALVES, chunk % HALVES
+
+        def one_source(source, carry):
+            first = (source * part + half * share) // SUB
+            subs = [first + i for i in range(share // SUB)]
+            ready = [scores(head, sub) for sub in subs]
+            for sub, parts in zip(subs, ready):
+                finish(head, sub, *parts)
+            out_copy(head, half, source).start()
             return carry
 
-        lax.fori_loop(0, tok // SUB // 2, pair, 0)
-        out_copy(chunk).start()
-    for chunk in range(CHUNKS):
-        out_copy(chunk).wait()
+        lax.fori_loop(0, tp, one_source, 0)
+    for chunk in range(chunks):
+        for source in range(tp):
+            out_copy(chunk // HALVES, chunk % HALVES, source).wait()
     for copy in sent:
         copy.wait_send()
 
@@ -302,7 +321,8 @@
     total = tok * count
     me = lax.axis_index("ctx").astype(jnp.int32)
     width = queries.shape[1] // tp
-    step = width // CHUNKS
+    step = width // heads
+    chunks = heads * HALVES
 
     per_dev = tok // SUB
     start = me * per_dev - slash_offsets // SUB - 1
@@ -325,8 +345,8 @@
         out_specs=hbm,
         scratch_shapes=[
             pltpu.VMEM((heads, total, 2 * DH), BF16),
-            pltpu.VMEM((CHUNKS, tok, step), BF16),
-            pltpu.VMEM((CHUNKS, tok, step), BF16),
+            pltpu.VMEM((heads, tok, step), BF16),
+            pltpu.VMEM((heads, tok, step), BF16),
             pltpu.VMEM((heads, vert_count, 2 * DH), F32),
             pltpu.VMEM((heads, vert_count, DH), BF16),
             pltpu.VMEM((heads, vert_count, 2 * DH), BF16),
@@ -337,12 +357,12 @@
             dma((heads, 2)),
             dma((tp - 1, heads, 2)),
             dma((tp - 1, heads, 2)),
-            dma((CHUNKS,)),
-            dma((tp - 1, CHUNKS)),
-            dma((tp - 1, CHUNKS)),
-            dma((heads, count)),
-            dma((heads, count)),
-            dma((CHUNKS,)),
+            dma((chunks,)),
+            dma((tp - 1, chunks)),
+            dma((tp - 1, chunks)),
+            dma((heads, count, tp)),
+            dma((heads, count, tp)),
+            dma((chunks, tp)),
         ],
         compiler_params=pltpu.CompilerParams(
             collective_id=0, has_side_effects=True, vmem_limit_bytes=VMEM_BYTES
@@ -351,7 +371,7 @@
             flops=scores * 1024, bytes_accessed=32 << 20, transcendentals=scores
         ),
         name="attend_all",
-    )(picks, queries, key_rows, value_rows, column, vertical_keys[:, None, :])
+    )(picks, queries, key_rows, value_rows, column, vertical_keys)
 
 
 def solution(mesh):

time: 151 us -> 139 us (0.921)
  Pallas kernels: 141 us -> 131 us
    pallas_call x1, Pallas kernels: 141 us -> 131 us  [shards(): pl.pallas_call(functools.partial(body, (tok, heads, bands, tp, count, ste...]
where the time goes in v2:
time: 139 us
  Pallas kernels  131 us (94%)
  local copies, waits for them, and re-layouts  6.87 us (5%)
  other arithmetic  1.52 us (1%)
    pallas_call x1, Pallas kernels, shards(): pl.pallas_call(functools.partial(body, (tok, heads, bands, tp, count, ste...  131 us
    unnamed x1, local copies, waits for them, and re-layouts  4.79 us

profile of v2, /device:TPU:0, one launch (start us, length us, event | category | flops | bytes accessed | tf_op | source)
XLA Modules:
  0.0 139.1 jit_solution(1610402644843970737)
XLA Ops:
  0.0 0.7 constant_dynamic-update-slice_fusion.5
  0.8 0.1 copy.7
  0.9 0.6 reshape.3.pick_ref
  1.5 0.7 fusion.1
  2.3 1.3 copy.8.column_ref
  3.6 130.7 %attend_all.1 = bf16[1024,2048]{1,0:T(8,128)(2,1)} custom-call(s32[36]{0:T(128)} %reshape.3.pick_ref, bf16[256,8192]{1,0:T(8,128)(2,1)} %q_hbm.1, bf16[256,1024]{1,0:T(8,128)(2,1)} %k_hbm.1, bf16[256,1024]{1,0:T(8,128)(2,1)} %v_hbm.1, s32[2,1024,1]{2,1,0:T(8,128)} %copy.8.column_ref, s32[2,1024]{1,0:T(2,128)} %row_ref.1), custom_call_target="tpu_custom_call" | custom-call | flops 25769803776 | bytes 33554432 | tf_op jit(solution)/shard_map/attend_all/pallas_call | solution.py:341
  134.3 4.8 %copy.15 = bf16[1024,2048]{1,0:T(8,128)(2,1)} copy(bf16[1024,2048]{1,0:T(8,128)(2,1)} %attend_all.1) | data formatting | bytes 8388608
  (5 shorter events, 0.1 us)

commit v3 on v2

--- a/solution.py
+++ b/solution.py
@@ -71,18 +71,19 @@
 
     def q_copy(k, chunk):
         head, half = chunk // HALVES, chunk % HALVES
-        first = pl.multiple_of((ring[k] * heads + head) * step, step)
+        other = lax.rem(me_t + k, tp)
+        first = pl.multiple_of((other * heads + head) * step, step)
         source = q_hbm.at[pl.ds(half * share, share), pl.ds(first, step)]
         landing = pl.multiple_of(me_t * part + half * share, share)
         target = qs.at[head, pl.ds(landing, share)]
-        if k == 0:
+        if isinstance(k, int) and k == 0:
             return pltpu.make_async_copy(source, target, q_loc.at[chunk])
         return pltpu.make_async_remote_copy(
             src_ref=source,
             dst_ref=target,
             send_sem=q_snd.at[k - 1, chunk],
             recv_sem=q_rcv.at[k - 1, chunk],
-            device_id=(me_c, ring[k]),
+            device_id=(me_c, other),
             device_id_type=MESH,
         )
 
@@ -101,7 +102,7 @@
     sent = []
 
     def start_q(chunk):
-        for k in range(tp - 1, 0, -1):
+        for k in range(1, tp):
             copy = q_copy(k, chunk)
             copy.start()
             sent.append(copy)
@@ -151,7 +152,8 @@
                 copy = ctx_copy(head, 0, bit, k)
                 copy.start()
                 sent.append(copy)
-    start_q(0)
+    for chunk in range(2):
+        start_q(chunk)
     for head in range(heads):
         add_vertical(head, 0)
     held = [[0] for _ in range(heads)]
@@ -165,19 +167,14 @@
                         copy = ctx_copy(head, fresh[head][index], bit, k)
                         copy.start()
                         sent.append(copy)
-        if turn < 2:
-            start_q(1 + turn)
+        if 2 + turn < chunks:
+            start_q(2 + turn)
         for head in range(heads):
             for slot in fresh[head]:
                 add_vertical(head, slot)
             held[head] += fresh[head]
-    for chunk in range(1 + min(bits, 2), chunks):
+    for chunk in range(2 + bits, chunks):
         start_q(chunk)
-
-    for head in range(heads):
-        vk[head] = vert_sum[head, :, :DH].astype(BF16)
-        vv[head, :, :DH] = vert_sum[head, :, DH:].astype(BF16)
-        vv[head, :, DH:] = jnp.ones((vv.shape[1], DH), BF16)
 
     per_dev = tok // SUB
     shifts = [1 << b for b in reversed(range(per_dev.bit_length() - 1))]
@@ -221,7 +218,10 @@
             both = lax.select(picks[2 + turn] == 1, moved, both)
         mark_win[head, band] = both
 
-    for head in range(heads):
+    def prepare(head):
+        vk[head] = vert_sum[head, :, :DH].astype(BF16)
+        vv[head, :, :DH] = vert_sum[head, :, DH:].astype(BF16)
+        vv[head, :, DH:] = jnp.ones((vv.shape[1], DH), BF16)
         for band in range(bands):
             cut_window(head, band)
 
@@ -288,22 +288,27 @@
             o_sem.at[head * HALVES + half, source],
         )
 
+    def one_source(head, half, source):
+        first = (source * part + half * share) // SUB
+        subs = [first + i for i in range(share // SUB)]
+        ready = [scores(head, sub) for sub in subs]
+        for sub, parts in zip(subs, ready):
+            finish(head, sub, *parts)
+        out_copy(head, half, source).start()
+
     for chunk in range(chunks):
+        head, half = chunk // HALVES, chunk % HALVES
+        if half == 0:
+            prepare(head)
         q_copy(0, chunk).wait()
-        for k in range(1, tp):
+        one_source(head, half, me_t)
+
+        def arrived(k, carry):
             q_copy(k, chunk).wait_recv()
-        head, half = chunk // HALVES, chunk % HALVES
-
-        def one_source(source, carry):
-            first = (source * part + half * share) // SUB
-            subs = [first + i for i in range(share // SUB)]
-            ready = [scores(head, sub) for sub in subs]
-            for sub, parts in zip(subs, ready):
-                finish(head, sub, *parts)
-            out_copy(head, half, source).start()
+            one_source(head, half, lax.rem(me_t - k + tp, tp))
             return carry
 
-        lax.fori_loop(0, tp, one_source, 0)
+        lax.fori_loop(1, tp, arrived, 0)
     for chunk in range(chunks):
         for source in range(tp):
             out_copy(chunk // HALVES, chunk % HALVES, source).wait()

time: 139 us -> 133 us (0.957)
  the two profiles are of different devices: /device:TPU:0 before, /device:TPU:30 now
where the time goes in v3:
time: 133 us
  Pallas kernels  125 us (94%)
  local copies, waits for them, and re-layouts  6.87 us (5%)
  other arithmetic  1.52 us (1%)
    pallas_call x1, Pallas kernels, shards(): pl.pallas_call(functools.partial(body, (tok, heads, bands, tp, count, ste...  125 us
    unnamed x1, local copies, waits for them, and re-layouts  4.79 us

profile of v3, /device:TPU:30, one launch (start us, length us, event | category | flops | bytes accessed | tf_op | source)
XLA Modules:
  0.0 133.2 jit_solution(6256115830472726242)
XLA Ops:
  0.0 0.7 constant_dynamic-update-slice_fusion.5
  0.8 0.1 copy.7
  0.9 0.6 reshape.3.pick_ref
  1.5 0.7 fusion.1
  2.3 1.3 %copy.8.column_ref = s32[2,1024,1]{2,1,0:T(8,128)} copy(s32[2,1024,1]{1,0,2:T(2,128)S(1)} %fusion.1) | data formatting | bytes 16384 | tf_op jit(solution)/shard_map/broadcast_in_dim | solution.py:339
  3.6 124.8 %attend_all.1 = bf16[1024,2048]{1,0:T(8,128)(2,1)} custom-call(s32[36]{0:T(128)} %reshape.3.pick_ref, bf16[256,8192]{1,0:T(8,128)(2,1)} %q_hbm.1, bf16[256,1024]{1,0:T(8,128)(2,1)} %k_hbm.1, bf16[256,1024]{1,0:T(8,128)(2,1)} %v_hbm.1, s32[2,1024,1]{2,1,0:T(8,128)} %copy.8.column_ref, s32[2,1024]{1,0:T(2,128)} %row_ref.1), custom_call_target="tpu_custom_call" | custom-call | flops 25769803776 | bytes 33554432 | tf_op jit(solution)/shard_map/attend_all/pallas_call | solution.py:346
  128.4 4.8 %copy.15 = bf16[1024,2048]{1,0:T(8,128)(2,1)} copy(bf16[1024,2048]{1,0:T(8,128)(2,1)} %attend_all.1) | data formatting | bytes 8388608
  (5 shorter events, 0.1 us)
